TPU v7x, 128 devices: a whole 4x4x4 slice. The times are simulated.
128 devices in a mesh: replica: 8 (over x, y_lo), fsdp: 16 (over y_hi, z, core).
Axes of the slice: x: 4, y: 4 (y_hi: 2, y_lo: 2; y = y_hi * 2 + y_lo), z: 4, core: 2. Of those that a mesh axis runs over, the one named last changes fastest.
Arguments:
- tokens: bfloat16 [16384, 4096], P(('replica', 'fsdp')), may hold values from -6 to 6
- up_cotangent: bfloat16 [16384, 16384], P('replica', 'fsdp'), may hold values from -6 to 6
- inner_up: bfloat16 [8, 4096, 16384], P('replica', None, 'fsdp'), may hold values from -6 to 6
- outer_up: float32 [4096, 16384], P('replica', 'fsdp'), may hold values from -6 to 6
- moment_up: float32 [4096, 16384], P('replica', 'fsdp'), may hold values from -4 to 4
Outputs:
- new_up: float32 [4096, 16384], P('replica', 'fsdp')
- new_moment_up: float32 [4096, 16384], P('replica', 'fsdp')
All inputs are finite; a program needn't handle non-finite values.
Results may differ from a plain program's by a relative error of at most 0.0003.
Values may be sent and summed in bfloat16 or wider, within the bound.
No kernel may reach another device: no remote copies, remote signals or barrier semaphores. Data moves between devices by JAX's collectives and lax.ppermute only.
A program may use at most 128 MiB of HBM per device.

v0:
```python
import math

import jax
import jax.numpy as jnp
from jax import lax
from jax.sharding import PartitionSpec as P


def dot_first(left, right):
    return lax.dot_general(
        left, right, (((0,), (0,)), ((), ())), preferred_element_type=jnp.float32
    )


def per_device(tokens, up_cotangent, inner_up, outer_up, moment_up):
    n_rep = lax.axis_size("replica")
    rep_rows = up_cotangent.shape[0]
    grad = dot_first(lax.all_gather(tokens, "fsdp", axis=0, tiled=True), up_cotangent)
    rate = 8.0 / math.sqrt(rep_rows)
    inner_new = inner_up[0].astype(jnp.float32) - rate * grad
    total = lax.psum(inner_new, "replica")
    share_rows = outer_up.shape[0]
    offset = lax.axis_index("replica") * share_rows
    share = lax.dynamic_slice_in_dim(total, offset, share_rows, 0)
    mean_inner = share / n_rep
    avg = outer_up - mean_inner
    new_moment = 0.9 * moment_up + avg
    new_up = outer_up - 0.7 * (avg + 0.9 * new_moment)
    return (new_up, new_moment)


def solution(mesh):
    placed = (
        P(("replica", "fsdp"), None),
        P("replica", "fsdp"),
        P("replica", None, "fsdp"),
        P("replica", "fsdp"),
        P("replica", "fsdp"),
    )
    return jax.shard_map(
        per_device,
        mesh=mesh,
        in_specs=placed,
        out_specs=(P("replica", "fsdp"), P("replica", "fsdp")),
        check_vma=False,
    )
```

profile of v0, /device:TPU:0, one launch (start us, length us, event | category | flops | bytes accessed | tf_op | source)
XLA Modules:
  0.0 812.0 jit_solution(9303749845745765876)
XLA Ops:
  7.2 0.0 all-gather.2.cloned.1.call-start
  7.2 0.7 all-gather.2.cloned.1.call-update
  7.9 0.0 all-reduce.2.cloned.1.call-start
  7.9 114.4 %all-gather.2.cloned.1.call-done = bf16[2048,4096]{1,0:T(8,128)(2,1)} async-done(((bf16[128,4096]{1,0:T(8,128)(2,1)}), bf16[2048,4096]{1,0:T(8,128)(2,1)}) %all-gather.2.cloned.1.call-update) | async-done | bytes 16777232 | tf_op jit(solution)/shard_map/all_gather | solution.py:18
  122.4 25.7 %convert_subtract_fusion = f32[4096,1024]{1,0:T(8,128)} fusion(bf16[2048,4096]{1,0:T(8,128)(2,1)} %all-gather.2.cloned.1.call-done, bf16[2048,1024]{1,0:T(8,128)(2,1)} %param.6, bf16[1,4096,1024]{2,1,0:T(8,128)(2,1)} %param.7), kind=kOutput, calls=%fused_computation | convolution fusion | flops 17192452096 | bytes 46137344 | tf_op jit(solution)/shard_map/dot_general | solution.py:10
  148.1 0.0 copy-start
  148.1 0.0 all-reduce.2.cloned.1.call-update
  148.1 651.8 %all-reduce.2.cloned.1.call-done = f32[4096,1024]{1,0:T(8,128)} async-done(((f32[4096,1024]{1,0:T(8,128)}), f32[4096,1024]{1,0:T(8,128)}) %all-reduce.2.cloned.1.call-update) | async-done | bytes 16777232 | tf_op jit(solution)/shard_map/psum | solution.py:21
  799.9 0.0 copy-done
  799.9 5.2 multiply_subtract_fusion
Async XLA Ops:
  7.2 115.2 %all-gather.2.cloned.1.call-start = ((), (), s32[]{:S(2)}) async-start(), calls=%async_computation | async-start | bytes 17825792 | tf_op jit(solution)/shard_map/all_gather | solution.py:18
  7.9 792.0 %all-reduce.2.cloned.1.call-start = ((), (), s32[]{:S(2)}) async-start(), calls=%async_computation.1 | async-start | bytes 33554432 | tf_op jit(solution)/shard_map/psum | solution.py:21
  148.1 651.8 %copy-start = (f32[512,1024]{1,0:T(8,128)S(1)}, f32[512,1024]{1,0:T(8,128)}, u32[]{:S(2)}) copy-start(f32[512,1024]{1,0:T(8,128)} %param.8) | copy-start | bytes 6291460
Sparse Core Ops, SparseCore 0:
  10.5 111.8 all-gather.1
  148.2 651.6 all-reduce.1
where the time goes:
time: 820 us; the launch traced here: 812 us
  waiting for transfers between devices  767 us (94%)
  matrix products  25.7 us (3%)
  between operations  14 us (2%)
    psum x1, waiting for transfers between devices, per_device(): total = lax.psum(inner_new, 'replica')  652 us
    all_gather x1, waiting for transfers between devices, per_device(): lax.all_gather(tokens, 'fsdp', axis=0, tiled=True)  114 us
    dot_general x1, matrix products, dot_first(): lax.dot_general(left, right, (((0,), (0,)), ((), ())), preferred_element_...  25.7 us
  transfers between devices with their start and end apart: 2, of which 2 were waited for; matrix products, arithmetic and copies ran while one was open for 0% of the time, Pallas kernels for 0%

commit v1 on v0

v1 whole, which is shorter than its diff:
```python
import math

import jax
import jax.numpy as jnp
from jax import lax
from jax.experimental import pallas as pl
from jax.experimental.pallas import tpu as pltpu
from jax.sharding import Mesh
from jax.sharding import PartitionSpec as P

AXES = ("x", "yl", "yh", "z", "c")
SIZES = (4, 2, 2, 4, 2)
WIRE = jnp.float16
GROUPS = (((2, 1),), ((1, 1), (3, 1)), ((0, 1), (2, 0)), ((1, 0), (3, 0)), ((0, 0),))


def shift(value, axis, by):
    n = lax.axis_size(axis)
    return lax.ppermute(value, axis, [(i, (i + by) % n) for i in range(n)])


def fan(value, axis):
    n = lax.axis_size(axis)
    pairs = [(2 * i + c, 2 * ((i + 1 - 2 * c) % n) + c) for i in range(n) for c in (0, 1)]
    return lax.ppermute(value, (axis, "c"), pairs)


def after(value, *others):
    return lax.optimization_barrier((value, *others))[0]


def dot_first(left, right):
    return lax.dot_general(
        left, right, (((0,), (0,)), ((), ())), preferred_element_type=jnp.float32
    )


def copy_block(index, block, out):
    out[...] = block[...]


def reorder(array, order, rows):
    width = array.shape[1]
    return pl.pallas_call(
        copy_block,
        grid_spec=pltpu.PrefetchScalarGridSpec(
            num_scalar_prefetch=1,
            grid=(len(order),),
            in_specs=[pl.BlockSpec((rows, width), lambda i, index: (index[i], 0))],
            out_specs=pl.BlockSpec((rows, width), lambda i, index: (i, 0)),
        ),
        out_shape=jax.ShapeDtypeStruct(array.shape, array.dtype),
    )(jnp.stack(order), array)


def per_device(tokens, up_cotangent, inner_up, outer_up, moment_up):
    x, yl, yh, z, c = [lax.axis_index(a) for a in AXES]
    rate = 8.0 / math.sqrt(up_cotangent.shape[0])
    own_tokens = tokens.shape[0]
    share = outer_up.shape[0]

    def at(dx, dy):
        return (((x + dx) % 4) * 2 + (yl + dy) % 2) * share

    def source(dc, dz, dy):
        return ((yh + dy) % 2) * 8 + ((z + dz) % 4) * 2 + (c + dc) % 2

    order = [source(dc, dz, dy) for dc in (0, 1) for dz in (0, 3, 1, 2) for dy in (0, 1)]
    cot = reorder(up_cotangent, order, own_tokens)

    blocks = [
        jnp.concatenate([lax.dynamic_slice_in_dim(tokens, at(*d), share, 1) for d in group], 1)
        for group in GROUPS
    ]
    first, second, rest = blocks[0], blocks[1], jnp.concatenate(blocks[2:], 1)
    first2, second2, rest2 = shift(first, "yh", 1), shift(second, "yh", 1), shift(rest, "yh", 1)
    others, start = [first2, second2], 0
    for b in blocks[2:]:
        others.append(rest2[:, start : start + b.shape[1]])
        start += b.shape[1]

    news = {}
    near = []
    for g, (own, other) in enumerate(zip(blocks, others)):
        pair = jnp.concatenate([own, other], 0)
        if g >= 2:
            pair = after(pair, *near[g - 2])
        below, above = shift(pair, "z", 1), shift(pair, "z", -1)
        near.append((below, above))
        beyond = fan(jnp.where(c == 0, below, above), "z")
        three = jnp.concatenate([pair, below, above], 0)
        all_tokens = jnp.concatenate([three, beyond, shift(three, "c", 1), shift(beyond, "c", 1)], 0)
        grad = dot_first(all_tokens, cot)
        for i, d in enumerate(GROUPS[g]):
            w = lax.dynamic_slice_in_dim(inner_up[0], at(*d), share, 0)
            news[d] = w.astype(jnp.float32) - rate * grad[i * share : (i + 1) * share]

    sums = {}
    for dy in (1, 0):
        far = fan(news[2, dy].astype(WIRE), "x").astype(jnp.float32)
        up = news[1, dy] + jnp.where(c == 0, far, 0.0)
        down = news[3, dy] + jnp.where(c == 1, far, 0.0)
        up = shift(up.astype(WIRE), "x", 1)
        down = shift(down.astype(WIRE), "x", -1)
        sums[dy] = news[0, dy] + up.astype(jnp.float32) + down.astype(jnp.float32)
    total = sums[0] + shift(sums[1].astype(WIRE), "yl", 1).astype(jnp.float32)
    mean_inner = total / 8
    avg = outer_up - mean_inner
    new_moment = 0.9 * moment_up + avg
    new_up = outer_up - 0.7 * (avg + 0.9 * new_moment)
    return (new_up, new_moment)


def solution(mesh):
    fine = Mesh(mesh.devices.reshape(SIZES), AXES)
    rep, fsdp = AXES[:2], AXES[2:]
    placed = (
        P(AXES, None),
        P(rep, fsdp),
        P(rep, None, fsdp),
        P(rep, fsdp),
        P(rep, fsdp),
    )
    return jax.shard_map(
        per_device,
        mesh=fine,
        in_specs=placed,
        out_specs=(P(rep, fsdp), P(rep, fsdp)),
        check_vma=False,
    )
```

time: 820 us -> 188 us (0.23)
  waiting for transfers between devices: 767 us -> 73.6 us
  starting transfers between devices: 0.08 us -> 47.9 us
  local copies, waits for them, and re-layouts: 0.01 us -> 18.1 us
  between operations: 14 us -> 1.19 us
  Pallas kernels: 0 us -> 10.8 us
    psum x1 -> x0, waiting for transfers between devices: 652 us -> none  [per_device(): total = lax.psum(inner_new, 'replica')]
    all_gather x1 -> x0, waiting for transfers between devices: 114 us -> none  [per_device(): lax.all_gather(tokens, 'fsdp', axis=0, tiled=True)]
    ppermute x0 -> x35, waiting for transfers between devices: none -> 73.6 us  [the longest x28 39.7 us: shift(): return lax.ppermute(value, axis, [(i, (i + by) % n) for i in range(n)])]
    ppermute x0 -> x35, starting transfers between devices: none -> 47.9 us  [the longest x28 40 us: shift(): return lax.ppermute(value, axis, [(i, (i + by) % n) for i in range(n)])]
    unnamed x2 -> x40, local copies, waits for them, and re-layouts: 0.01 us -> 13.8 us
    pallas_call x0 -> x1, Pallas kernels: none -> 10.8 us  [reorder(): pl.pallas_call(copy_block, grid_spec=pltpu.PrefetchScalarGridSpec(num_sca...]
    dot_general x1 -> x5, matrix products: 25.7 us -> 28.5 us  [dot_first(): lax.dot_general(left, right, (((0,), (0,)), ((), ())), preferred_element_...]
  transfers between devices with their start and end apart: 2 -> 35, of which waited for: 2 -> 17; matrix products, arithmetic and copies ran while one was open for 0% -> 23% of each run, Pallas kernels for 0% -> 6%
where the time goes in v1:
time: 188 us; the launch traced here: 187 us
  waiting for transfers between devices  73.6 us (39%)
  starting transfers between devices  47.9 us (25%)
  matrix products  28.5 us (15%)
  local copies, waits for them, and re-layouts  18.1 us (10%)
  Pallas kernels  10.8 us (6%)
  other arithmetic  7.16 us (4%)
    ppermute x28, starting transfers between devices, shift(): return lax.ppermute(value, axis, [(i, (i + by) % n) for i in range(n)])  40 us
    ppermute x28, waiting for transfers between devices, shift(): return lax.ppermute(value, axis, [(i, (i + by) % n) for i in range(n)])  39.7 us
    ppermute x7, waiting for transfers between devices, fan(): return lax.ppermute(value, (axis, 'c'), pairs)  33.9 us
    dot_general x5, matrix products, dot_first(): lax.dot_general(left, right, (((0,), (0,)), ((), ())), preferred_element_...  28.5 us
    unnamed x40, local copies, waits for them, and re-layouts  13.8 us
    pallas_call x1, Pallas kernels, reorder(): pl.pallas_call(copy_block, grid_spec=pltpu.PrefetchScalarGridSpec(num_sca...  10.8 us
    ppermute x7, starting transfers between devices, fan(): return lax.ppermute(value, (axis, 'c'), pairs)  7.86 us
  transfers between devices with their start and end apart: 35, of which 17 were waited for; matrix products, arithmetic and copies ran while one was open for 23% of the time, Pallas kernels for 6%

profile of v1, /device:TPU:0, one launch (start us, length us, event | category | flops | bytes accessed | tf_op | source)
XLA Modules:
  0.0 187.3 jit_solution(3916258277210885660)
XLA Ops:
  5.4 3.3 %collective-permute-start.1 = (bf16[128,512]{1,0:T(8,128)(2,1)S(1)}, bf16[128,512]{1,0:T(8,128)(2,1)S(1)}, u32[]{:S(2)}, u32[]{:S(2)}) collective-permute-start(bf16[128,512]{1,0:T(8,128)(2,1)S(1)} %get-tuple-element.11), channel_id=1, source_target_pairs={{0,8},{8,0},{1,9},{9,1},{2,10},{10,2},{3,11},{11,3},{4,12},{12,4},... | collective-permute-start | bytes 393224 | tf_op jit(solution)/shard_map/ppermute | solution.py:19
  10.6 3.4 %collective-permute-start = (bf16[128,2560]{1,0:T(8,128)(2,1)S(1)}, bf16[128,2560]{1,0:T(8,128)(2,1)S(1)}, u32[]{:S(2)}, u32[]{:S(2)}) collective-permute-start(bf16[128,2560]{1,0:T(8,128)(2,1)S(1)} %get-tuple-element.12), channel_id=1, source_target_pairs={{0,8},{8,0},{1,9},{9,1},{2,10},{10,2},{3,11},{11,3},{4,12},{12,4},... | collective-permute-start | bytes 1966088 | tf_op jit(solution)/shard_map/ppermute | solution.py:19
  14.6 10.8 %shard_map.68 = bf16[2048,1024]{1,0:T(8,128)(2,1)} custom-call(s32[16]{0:T(128)} %stack.67.index, bf16[2048,1024]{1,0:T(8,128)(2,1)} %block.1), custom_call_target="tpu_custom_call" | custom-call | tf_op jit(solution)/shard_map/pallas_call | solution.py:44
  30.5 3.2 %collective-permute-start.13 = (bf16[256,1024]{1,0:T(8,128)(2,1)S(1)}, bf16[256,1024]{1,0:T(8,128)(2,1)S(1)}, u32[]{:S(2)}, u32[]{:S(2)}) collective-permute-start(bf16[256,1024]{1,0:T(8,128)(2,1)S(1)} %pad_maximum_fusion.7), channel_id=1, source_target_pairs={{0,6},{2,0},{4,2},{6,4},{1,7},{3,1},{5,3},{7,5},{8,14},{10,8},{12,... | collective-permute-start | bytes 1572872 | tf_op jit(solution)/shard_map/ppermute | solution.py:19
  34.4 2.4 %collective-permute-done.2 = bf16[256,512]{1,0:T(8,128)(2,1)S(1)} collective-permute-done((bf16[256,512]{1,0:T(8,128)(2,1)S(1)}, bf16[256,512]{1,0:T(8,128)(2,1)S(1)}, u32[]{:S(2)}, u32[]{:S(2)}) %collective-permute-start.2) | collective-permute-done | bytes 262176 | tf_op jit(solution)/shard_map/ppermute | solution.py:19
  41.5 12.2 %collective-permute-done.28 = bf16[256,512]{1,0:T(8,128)(2,1)S(1)} collective-permute-done((bf16[256,512]{1,0:T(8,128)(2,1)S(1)}, bf16[256,512]{1,0:T(8,128)(2,1)S(1)}, u32[]{:S(2)}, u32[]{:S(2)}) %collective-permute-start.28) | collective-permute-done | bytes 262176 | tf_op jit(solution)/shard_map/ppermute | solution.py:25
  57.9 2.6 %collective-permute-done.4 = bf16[256,1024]{1,0:T(8,128)(2,1)S(1)} collective-permute-done((bf16[256,1024]{1,0:T(8,128)(2,1)S(1)}, bf16[256,1024]{1,0:T(8,128)(2,1)S(1)}, u32[]{:S(2)}, u32[]{:S(2)}) %collective-permute-start.4) | collective-permute-done | bytes 524320 | tf_op jit(solution)/shard_map/ppermute | solution.py:19
  60.5 4.3 %collective-permute-start.15 = (bf16[256,1024]{1,0:T(8,128)(2,1)S(1)}, bf16[256,1024]{1,0:T(8,128)(2,1)S(1)}, u32[]{:S(2)}, u32[]{:S(2)}) collective-permute-start(bf16[256,1024]{1,0:T(8,128)(2,1)S(1)} %pad_maximum_fusion.6), channel_id=1, source_target_pairs={{0,6},{2,0},{4,2},{6,4},{1,7},{3,1},{5,3},{7,5},{8,14},{10,8},{12,... | collective-permute-start | bytes 1572872 | tf_op jit(solution)/shard_map/ppermute | solution.py:19
  65.1 2.5 %collective-permute-start.25 = (bf16[256,1024]{1,0:T(8,128)(2,1)S(1)}, bf16[256,1024]{1,0:T(8,128)(2,1)S(1)}, u32[]{:S(2)}, u32[]{:S(2)}) collective-permute-start(bf16[256,1024]{1,0:T(8,128)(2,1)S(1)} %get-tuple-element.36), channel_id=1, source_target_pairs={{0,2},{1,7},{2,4},{3,1},{4,6},{5,3},{6,0},{7,5},{8,10},{9,15},{10,... | collective-permute-start | bytes 1572872 | tf_op jit(solution)/shard_map/ppermute | solution.py:25
  68.3 3.6 %fusion.18 = f16[512,1024]{1,0:T(8,128)(2,1)S(1)} fusion(bf16[2048,512]{1,0:T(8,128)(2,1)S(1)} %constant_dynamic-update-slice_fusion.30, bf16[2048,1024]{1,0:T(8,128)(2,1)S(1)} %copy-done, bf16[1,4096,1024]{2,1,0:T(8,128)(2,1)} %param.7, s32[]{:T(128)S(6)} %select_n.284), kind=kOutput, calls=%fused_computation.29 | convolution fusion | flops 2149580800 | bytes 8388612 | tf_op jit(solution)/shard_map/dot_general | solution.py:33
  72.4 2.7 %collective-permute-start.7 = (bf16[256,512]{1,0:T(8,128)(2,1)S(1)}, bf16[256,512]{1,0:T(8,128)(2,1)S(1)}, u32[]{:S(2)}, u32[]{:S(2)}) collective-permute-start(bf16[256,512]{1,0:T(8,128)(2,1)S(1)} %pad_maximum_fusion.8), channel_id=1, source_target_pairs={{0,6},{2,0},{4,2},{6,4},{1,7},{3,1},{5,3},{7,5},{8,14},{10,8},{12,... | collective-permute-start | bytes 786440 | tf_op jit(solution)/shard_map/ppermute | solution.py:19
  82.8 4.5 %collective-permute-start.20 = (bf16[768,1024]{1,0:T(8,128)(2,1)S(1)}, bf16[768,1024]{1,0:T(8,128)(2,1)S(1)}, u32[]{:S(2)}, u32[]{:S(2)}) collective-permute-start(bf16[768,1024]{1,0:T(8,128)(2,1)S(1)} %pad_maximum_fusion.1), channel_id=1, source_target_pairs={{0,1},{1,0},{2,3},{3,2},{4,5},{5,4},{6,7},{7,6},{8,9},{9,8},{10,11... | collective-permute-start | bytes 4718600 | tf_op jit(solution)/shard_map/ppermute | solution.py:19
  90.0 4.1 %collective-permute-done.16 = bf16[256,1024]{1,0:T(8,128)(2,1)S(1)} collective-permute-done((bf16[256,1024]{1,0:T(8,128)(2,1)S(1)}, bf16[256,1024]{1,0:T(8,128)(2,1)S(1)}, u32[]{:S(2)}, u32[]{:S(2)}) %collective-permute-start.16) | collective-permute-done | bytes 524320 | tf_op jit(solution)/shard_map/ppermute | solution.py:25
  94.0 3.1 %collective-permute-start.17 = (bf16[768,1024]{1,0:T(8,128)(2,1)S(1)}, bf16[768,1024]{1,0:T(8,128)(2,1)S(1)}, u32[]{:S(2)}, u32[]{:S(2)}) collective-permute-start(bf16[768,1024]{1,0:T(8,128)(2,1)S(1)} %pad_maximum_fusion), channel_id=1, source_target_pairs={{0,1},{1,0},{2,3},{3,2},{4,5},{5,4},{6,7},{7,6},{8,9},{9,8},{10,11... | collective-permute-start | bytes 4718600 | tf_op jit(solution)/shard_map/ppermute | solution.py:19
  100.5 6.9 %fusion.27 = f32[1024,1024]{1,0:T(8,128)S(1)} fusion(bf16[2048,1024]{1,0:T(8,128)(2,1)} %constant_dynamic-update-slice_fusion.23, bf16[2048,1024]{1,0:T(8,128)(2,1)S(1)} %copy-done), kind=kOutput, calls=%fused_computation.102 | convolution fusion | flops 4294967296 | bytes 12582912 | tf_op jit(solution)/shard_map/dot_general | solution.py:33
  109.1 2.8 %collective-permute-start.33 = (f16[512,1024]{1,0:T(8,128)(2,1)S(1)}, f16[512,1024]{1,0:T(8,128)(2,1)S(1)}, u32[]{:S(2)}, u32[]{:S(2)}) collective-permute-start(f16[512,1024]{1,0:T(8,128)(2,1)S(1)} %get-tuple-element.25), channel_id=1, source_target_pairs={{0,96},{32,0},{64,32},{96,64},{1,97},{33,1},{65,33},{97,65},{2,98}... | collective-permute-start | bytes 3145736 | tf_op jit(solution)/shard_map/ppermute | solution.py:19
  114.1 6.3 %fusion.26 = f32[1024,1024]{1,0:T(8,128)S(1)} fusion(bf16[2048,1024]{1,0:T(8,128)(2,1)} %constant_dynamic-update-slice_fusion.17, bf16[2048,1024]{1,0:T(8,128)(2,1)S(1)} %copy-done), kind=kOutput, calls=%fused_computation.101 | convolution fusion | flops 4294967296 | bytes 12582912 | tf_op jit(solution)/shard_map/dot_general | solution.py:33
  122.7 11.9 %collective-permute-done.33 = f16[512,1024]{1,0:T(8,128)(2,1)S(1)} collective-permute-done((f16[512,1024]{1,0:T(8,128)(2,1)S(1)}, f16[512,1024]{1,0:T(8,128)(2,1)S(1)}, u32[]{:S(2)}, u32[]{:S(2)}) %collective-permute-start.33) | collective-permute-done | bytes 1048608 | tf_op jit(solution)/shard_map/ppermute | solution.py:19
  134.6 4.7 %collective-permute-done.32 = f16[512,1024]{1,0:T(8,128)(2,1)S(1)} collective-permute-done((f16[512,1024]{1,0:T(8,128)(2,1)S(1)}, f16[512,1024]{1,0:T(8,128)(2,1)S(1)}, u32[]{:S(2)}, u32[]{:S(2)}) %collective-permute-start.32) | collective-permute-done | bytes 1048608 | tf_op jit(solution)/shard_map/ppermute | solution.py:19
  140.7 6.3 %fusion.25 = f32[1024,1024]{1,0:T(8,128)S(1)} fusion(bf16[2048,1024]{1,0:T(8,128)(2,1)} %constant_dynamic-update-slice_fusion.11, bf16[2048,1024]{1,0:T(8,128)(2,1)S(1)} %copy-done), kind=kOutput, calls=%fused_computation.100 | convolution fusion | flops 4294967296 | bytes 12582912 | tf_op jit(solution)/shard_map/dot_general | solution.py:33
  147.7 8.9 %collective-permute-done.22 = f16[512,1024]{1,0:T(8,128)(2,1)S(1)} collective-permute-done((f16[512,1024]{1,0:T(8,128)(2,1)S(1)}, f16[512,1024]{1,0:T(8,128)(2,1)S(1)}, u32[]{:S(2)}, u32[]{:S(2)}) %collective-permute-start.22) | collective-permute-done | bytes 1048608 | tf_op jit(solution)/shard_map/ppermute | solution.py:25
  161.1 6.7 %collective-permute-done.8 = bf16[256,512]{1,0:T(8,128)(2,1)S(1)} collective-permute-done((bf16[256,512]{1,0:T(8,128)(2,1)S(1)}, bf16[256,512]{1,0:T(8,128)(2,1)S(1)}, u32[]{:S(2)}, u32[]{:S(2)}) %collective-permute-start.8) | collective-permute-done | bytes 262176 | tf_op jit(solution)/shard_map/ppermute | solution.py:25
  171.0 8.7 %collective-permute-done.24 = f16[512,1024]{1,0:T(8,128)(2,1)S(1)} collective-permute-done((f16[512,1024]{1,0:T(8,128)(2,1)S(1)}, f16[512,1024]{1,0:T(8,128)(2,1)S(1)}, u32[]{:S(2)}, u32[]{:S(2)}) %collective-permute-start.24) | collective-permute-done | bytes 1048608 | tf_op jit(solution)/shard_map/ppermute | solution.py:19
  181.9 5.4 %multiply_subtract_fusion = (f32[512,1024]{1,0:T(8,128)}, f32[512,1024]{1,0:T(8,128)}) fusion(f32[512,1024]{1,0:T(8,128)S(1)} %copy-done.1, f32[512,1024]{1,0:T(8,128)S(1)} %copy-done.2, f16[512,1024]{1,0:T(8,128)(2,1)S(1)} %collective-permute-done.34, f16[512,1024]{1,0:T(8,128)(2,1)S(1)} %collective-permute-done.24, ...), kind=kOutput, calls=%fused_computation.36 | convolution fusion | flops 2156396544 | bytes 18874372 | tf_op jit(solution)/shard_map/dot_general | solution.py:33
  (121 shorter events, 54.8 us)
Async XLA Ops:
  5.4 20.1 %collective-permute-start.1 = (bf16[128,512]{1,0:T(8,128)(2,1)S(1)}, bf16[128,512]{1,0:T(8,128)(2,1)S(1)}, u32[]{:S(2)}, u32[]{:S(2)}) collective-permute-start(bf16[128,512]{1,0:T(8,128)(2,1)S(1)} %get-tuple-element.11), channel_id=1, source_target_pairs={{0,8},{8,0},{1,9},{9,1},{2,10},{10,2},{3,11},{11,3},{4,12},{12,4},... | collective-permute-start | bytes 393224 | tf_op jit(solution)/shard_map/ppermute | solution.py:19
  9.4 20.9 %collective-permute-start.11 = (bf16[128,1024]{1,0:T(8,128)(2,1)S(1)}, bf16[128,1024]{1,0:T(8,128)(2,1)S(1)}, u32[]{:S(2)}, u32[]{:S(2)}) collective-permute-start(bf16[128,1024]{1,0:T(8,128)(2,1)S(1)} %get-tuple-element.42), channel_id=1, source_target_pairs={{0,8},{8,0},{1,9},{9,1},{2,10},{10,2},{3,11},{11,3},{4,12},{12,4},... | collective-permute-start | bytes 786440 | tf_op jit(solution)/shard_map/ppermute | solution.py:19
  10.6 29.0 %collective-permute-start = (bf16[128,2560]{1,0:T(8,128)(2,1)S(1)}, bf16[128,2560]{1,0:T(8,128)(2,1)S(1)}, u32[]{:S(2)}, u32[]{:S(2)}) collective-permute-start(bf16[128,2560]{1,0:T(8,128)(2,1)S(1)} %get-tuple-element.12), channel_id=1, source_target_pairs={{0,8},{8,0},{1,9},{9,1},{2,10},{10,2},{3,11},{11,3},{4,12},{12,4},... | collective-permute-start | bytes 1966088 | tf_op jit(solution)/shard_map/ppermute | solution.py:19
  30.4 25.3 %collective-permute-start.12 = (bf16[256,1024]{1,0:T(8,128)(2,1)S(1)}, bf16[256,1024]{1,0:T(8,128)(2,1)S(1)}, u32[]{:S(2)}, u32[]{:S(2)}) collective-permute-start(bf16[256,1024]{1,0:T(8,128)(2,1)S(1)} %pad_maximum_fusion.7), channel_id=1, source_target_pairs={{0,2},{2,4},{4,6},{6,0},{1,3},{3,5},{5,7},{7,1},{8,10},{10,12},{12... | collective-permute-start | bytes 1572872 | tf_op jit(solution)/shard_map/ppermute | solution.py:19
  30.5 25.4 %collective-permute-start.13 = (bf16[256,1024]{1,0:T(8,128)(2,1)S(1)}, bf16[256,1024]{1,0:T(8,128)(2,1)S(1)}, u32[]{:S(2)}, u32[]{:S(2)}) collective-permute-start(bf16[256,1024]{1,0:T(8,128)(2,1)S(1)} %pad_maximum_fusion.7), channel_id=1, source_target_pairs={{0,6},{2,0},{4,2},{6,4},{1,7},{3,1},{5,3},{7,5},{8,14},{10,8},{12,... | collective-permute-start | bytes 1572872 | tf_op jit(solution)/shard_map/ppermute | solution.py:19
  38.3 15.4 %collective-permute-start.28 = (bf16[256,512]{1,0:T(8,128)(2,1)S(1)}, bf16[256,512]{1,0:T(8,128)(2,1)S(1)}, u32[]{:S(2)}, u32[]{:S(2)}) collective-permute-start(bf16[256,512]{1,0:T(8,128)(2,1)S(1)} %get-tuple-element.44), channel_id=1, source_target_pairs={{0,2},{1,7},{2,4},{3,1},{4,6},{5,3},{6,0},{7,5},{8,10},{9,15},{10,... | collective-permute-start | bytes 786440 | tf_op jit(solution)/shard_map/ppermute | solution.py:25
  39.5 28.1 %collective-permute-start.29 = (bf16[768,512]{1,0:T(8,128)(2,1)S(1)}, bf16[768,512]{1,0:T(8,128)(2,1)S(1)}, u32[]{:S(2)}, u32[]{:S(2)}) collective-permute-start(bf16[768,512]{1,0:T(8,128)(2,1)S(1)} %pad_maximum_fusion.4), channel_id=1, source_target_pairs={{0,1},{1,0},{2,3},{3,2},{4,5},{5,4},{6,7},{7,6},{8,9},{9,8},{10,11... | collective-permute-start | bytes 2359304 | tf_op jit(solution)/shard_map/ppermute | solution.py:19
  39.7 20.8 %collective-permute-start.4 = (bf16[256,1024]{1,0:T(8,128)(2,1)S(1)}, bf16[256,1024]{1,0:T(8,128)(2,1)S(1)}, u32[]{:S(2)}, u32[]{:S(2)}) collective-permute-start(bf16[256,1024]{1,0:T(8,128)(2,1)S(1)} %pad_maximum_fusion.5), channel_id=1, source_target_pairs={{0,2},{2,4},{4,6},{6,0},{1,3},{3,5},{5,7},{7,1},{8,10},{10,12},{12... | collective-permute-start | bytes 1572872 | tf_op jit(solution)/shard_map/ppermute | solution.py:19
  55.8 16.5 %collective-permute-start.14 = (bf16[256,1024]{1,0:T(8,128)(2,1)S(1)}, bf16[256,1024]{1,0:T(8,128)(2,1)S(1)}, u32[]{:S(2)}, u32[]{:S(2)}) collective-permute-start(bf16[256,1024]{1,0:T(8,128)(2,1)S(1)} %pad_maximum_fusion.6), channel_id=1, source_target_pairs={{0,2},{2,4},{4,6},{6,0},{1,3},{3,5},{5,7},{7,1},{8,10},{10,12},{12... | collective-permute-start | bytes 1572872 | tf_op jit(solution)/shard_map/ppermute | solution.py:19
  60.5 16.7 %collective-permute-start.15 = (bf16[256,1024]{1,0:T(8,128)(2,1)S(1)}, bf16[256,1024]{1,0:T(8,128)(2,1)S(1)}, u32[]{:S(2)}, u32[]{:S(2)}) collective-permute-start(bf16[256,1024]{1,0:T(8,128)(2,1)S(1)} %pad_maximum_fusion.6), channel_id=1, source_target_pairs={{0,6},{2,0},{4,2},{6,4},{1,7},{3,1},{5,3},{7,5},{8,14},{10,8},{12,... | collective-permute-start | bytes 1572872 | tf_op jit(solution)/shard_map/ppermute | solution.py:19
  65.1 14.9 %collective-permute-start.25 = (bf16[256,1024]{1,0:T(8,128)(2,1)S(1)}, bf16[256,1024]{1,0:T(8,128)(2,1)S(1)}, u32[]{:S(2)}, u32[]{:S(2)}) collective-permute-start(bf16[256,1024]{1,0:T(8,128)(2,1)S(1)} %get-tuple-element.36), channel_id=1, source_target_pairs={{0,2},{1,7},{2,4},{3,1},{4,6},{5,3},{6,0},{7,5},{8,10},{9,15},{10,... | collective-permute-start | bytes 1572872 | tf_op jit(solution)/shard_map/ppermute | solution.py:25
  67.5 29.6 %collective-permute-start.26 = (bf16[768,1024]{1,0:T(8,128)(2,1)S(1)}, bf16[768,1024]{1,0:T(8,128)(2,1)S(1)}, u32[]{:S(2)}, u32[]{:S(2)}) collective-permute-start(bf16[768,1024]{1,0:T(8,128)(2,1)S(1)} %pad_maximum_fusion.2), channel_id=1, source_target_pairs={{0,1},{1,0},{2,3},{3,2},{4,5},{5,4},{6,7},{7,6},{8,9},{9,8},{10,11... | collective-permute-start | bytes 4718600 | tf_op jit(solution)/shard_map/ppermute | solution.py:19
  67.6 15.2 %collective-permute-start.6 = (bf16[256,512]{1,0:T(8,128)(2,1)S(1)}, bf16[256,512]{1,0:T(8,128)(2,1)S(1)}, u32[]{:S(2)}, u32[]{:S(2)}) collective-permute-start(bf16[256,512]{1,0:T(8,128)(2,1)S(1)} %pad_maximum_fusion.8), channel_id=1, source_target_pairs={{0,2},{2,4},{4,6},{6,0},{1,3},{3,5},{5,7},{7,1},{8,10},{10,12},{12... | collective-permute-start | bytes 786440 | tf_op jit(solution)/shard_map/ppermute | solution.py:19
  72.4 15.0 %collective-permute-start.7 = (bf16[256,512]{1,0:T(8,128)(2,1)S(1)}, bf16[256,512]{1,0:T(8,128)(2,1)S(1)}, u32[]{:S(2)}, u32[]{:S(2)}) collective-permute-start(bf16[256,512]{1,0:T(8,128)(2,1)S(1)} %pad_maximum_fusion.8), channel_id=1, source_target_pairs={{0,6},{2,0},{4,2},{6,4},{1,7},{3,1},{5,3},{7,5},{8,14},{10,8},{12,... | collective-permute-start | bytes 786440 | tf_op jit(solution)/shard_map/ppermute | solution.py:19
  82.8 26.3 %collective-permute-start.20 = (bf16[768,1024]{1,0:T(8,128)(2,1)S(1)}, bf16[768,1024]{1,0:T(8,128)(2,1)S(1)}, u32[]{:S(2)}, u32[]{:S(2)}) collective-permute-start(bf16[768,1024]{1,0:T(8,128)(2,1)S(1)} %pad_maximum_fusion.1), channel_id=1, source_target_pairs={{0,1},{1,0},{2,3},{3,2},{4,5},{5,4},{6,7},{7,6},{8,9},{9,8},{10,11... | collective-permute-start | bytes 4718600 | tf_op jit(solution)/shard_map/ppermute | solution.py:19
  88.4 19.0 %collective-permute-start.31 = (f16[512,1024]{1,0:T(8,128)(2,1)S(1)}, f16[512,1024]{1,0:T(8,128)(2,1)S(1)}, u32[]{:S(2)}, u32[]{:S(2)}) collective-permute-start(f16[512,1024]{1,0:T(8,128)(2,1)S(1)} %fusion.18), channel_id=1, source_target_pairs={{0,32},{1,97},{32,64},{33,1},{64,96},{65,33},{96,0},{97,65},{2,34}... | collective-permute-start | bytes 3145736 | tf_op jit(solution)/shard_map/ppermute | solution.py:25
  94.0 26.4 %collective-permute-start.17 = (bf16[768,1024]{1,0:T(8,128)(2,1)S(1)}, bf16[768,1024]{1,0:T(8,128)(2,1)S(1)}, u32[]{:S(2)}, u32[]{:S(2)}) collective-permute-start(bf16[768,1024]{1,0:T(8,128)(2,1)S(1)} %pad_maximum_fusion), channel_id=1, source_target_pairs={{0,1},{1,0},{2,3},{3,2},{4,5},{5,4},{6,7},{7,6},{8,9},{9,8},{10,11... | collective-permute-start | bytes 4718600 | tf_op jit(solution)/shard_map/ppermute | solution.py:19
  97.2 70.7 %collective-permute-start.9 = (bf16[768,512]{1,0:T(8,128)(2,1)S(1)}, bf16[768,512]{1,0:T(8,128)(2,1)S(1)}, u32[]{:S(2)}, u32[]{:S(2)}) collective-permute-start(bf16[768,512]{1,0:T(8,128)(2,1)S(1)} %pad_maximum_fusion.3), channel_id=1, source_target_pairs={{0,1},{1,0},{2,3},{3,2},{4,5},{5,4},{6,7},{7,6},{8,9},{9,8},{10,11... | collective-permute-start | bytes 2359304 | tf_op jit(solution)/shard_map/ppermute | solution.py:19
  109.1 25.5 %collective-permute-start.33 = (f16[512,1024]{1,0:T(8,128)(2,1)S(1)}, f16[512,1024]{1,0:T(8,128)(2,1)S(1)}, u32[]{:S(2)}, u32[]{:S(2)}) collective-permute-start(f16[512,1024]{1,0:T(8,128)(2,1)S(1)} %get-tuple-element.25), channel_id=1, source_target_pairs={{0,96},{32,0},{64,32},{96,64},{1,97},{33,1},{65,33},{97,65},{2,98}... | collective-permute-start | bytes 3145736 | tf_op jit(solution)/shard_map/ppermute | solution.py:19
  113.2 26.1 %collective-permute-start.32 = (f16[512,1024]{1,0:T(8,128)(2,1)S(1)}, f16[512,1024]{1,0:T(8,128)(2,1)S(1)}, u32[]{:S(2)}, u32[]{:S(2)}) collective-permute-start(f16[512,1024]{1,0:T(8,128)(2,1)S(1)} %get-tuple-element.24), channel_id=1, source_target_pairs={{0,32},{32,64},{64,96},{96,0},{1,33},{33,65},{65,97},{97,1},{2,34}... | collective-permute-start | bytes 3145736 | tf_op jit(solution)/shard_map/ppermute | solution.py:19
  140.6 16.1 %collective-permute-start.22 = (f16[512,1024]{1,0:T(8,128)(2,1)S(1)}, f16[512,1024]{1,0:T(8,128)(2,1)S(1)}, u32[]{:S(2)}, u32[]{:S(2)}) collective-permute-start(f16[512,1024]{1,0:T(8,128)(2,1)S(1)} %get-tuple-element.26), channel_id=1, source_target_pairs={{0,32},{1,97},{32,64},{33,1},{64,96},{65,33},{96,0},{97,65},{2,34}... | collective-permute-start | bytes 3145736 | tf_op jit(solution)/shard_map/ppermute | solution.py:25
  147.0 24.1 %collective-permute-start.34 = (f16[512,1024]{1,0:T(8,128)(2,1)S(1)}, f16[512,1024]{1,0:T(8,128)(2,1)S(1)}, u32[]{:S(2)}, u32[]{:S(2)}) collective-permute-start(f16[512,1024]{1,0:T(8,128)(2,1)S(1)} %get-tuple-element.27), channel_id=1, source_target_pairs={{0,16},{16,0},{1,17},{17,1},{2,18},{18,2},{3,19},{19,3},{4,20},{20... | collective-permute-start | bytes 3145736 | tf_op jit(solution)/shard_map/ppermute | solution.py:19
  157.8 22.0 %collective-permute-start.24 = (f16[512,1024]{1,0:T(8,128)(2,1)S(1)}, f16[512,1024]{1,0:T(8,128)(2,1)S(1)}, u32[]{:S(2)}, u32[]{:S(2)}) collective-permute-start(f16[512,1024]{1,0:T(8,128)(2,1)S(1)} %get-tuple-element.23), channel_id=1, source_target_pairs={{0,96},{32,0},{64,32},{96,64},{1,97},{33,1},{65,33},{97,65},{2,98}... | collective-permute-start | bytes 3145736 | tf_op jit(solution)/shard_map/ppermute | solution.py:19
  157.9 24.0 %collective-permute-start.23 = (f16[512,1024]{1,0:T(8,128)(2,1)S(1)}, f16[512,1024]{1,0:T(8,128)(2,1)S(1)}, u32[]{:S(2)}, u32[]{:S(2)}) collective-permute-start(f16[512,1024]{1,0:T(8,128)(2,1)S(1)} %get-tuple-element.22), channel_id=1, source_target_pairs={{0,32},{32,64},{64,96},{96,0},{1,33},{33,65},{65,97},{97,1},{2,34}... | collective-permute-start | bytes 3145736 | tf_op jit(solution)/shard_map/ppermute | solution.py:19
  (19 other events, 216.3 us)
